TPU v7x, 32 devices: a whole 2x2x4 slice. The times are simulated.
32 devices in a mesh: wind: 2 (over y), gx: 4 (over z), gy: 2 (over x), gz: 2 (over core).
Axes of the slice: x: 2, y: 2, z: 4, core: 2. Of those that a mesh axis runs over, the one named last changes fastest.
Arguments:
- pressure: bfloat16 [8192, 8192], P(('wind', 'gx'), ('gy', 'gz')), parts along dimension 0, may hold values from -40 to 40
- fir_taps: bfloat16 [257], replicated, may hold values from -0.375 to 0.375
- influence: bfloat16 [256, 4, 4, 512], P(None, ('gy', 'gz'), 'gx'), may hold values from -0.0625 to 0.0625
- mode_impulse: float32 [256, 64], replicated, may hold values from -0.75 to 0.75
- mode_taps: int32 [256], replicated, may hold values from 1 to 64, as said below
Outputs:
- responses: bfloat16 [512, 4096], P(('wind', 'gx', 'gy', 'gz')), parts along dimension 0
- correlation_score: float32 [512, 4, 4, 512], P('wind', ('gy', 'gz'), 'gx'), parts along dimension 0
There are 2 independent parts, one for each index of `wind`. A program takes and returns all parts, laid end to end along the dimension named above; an argument that names none is the same for every part. Nothing has to cross between parts.
Inputs may be any that keep to these rules, and one draw needn't show every extreme that they name: `mode_taps`: some mode keeps all 64 taps.
All inputs are finite; a program needn't handle non-finite values.
Results may differ from a plain program's by a relative error of at most 0.005.
Values may be sent and summed in bfloat16 or wider, within the bound.
A program may use at most 64 MiB of HBM per device.

v0:
```python
import math
import jax
import jax.numpy as jnp
from jax import lax
from jax.sharding import PartitionSpec as P


def band_matrix(tap_row, row_count):
    tap_count = tap_row.shape[0]
    extended = jnp.concatenate([tap_row[::-1], jnp.zeros((row_count,), tap_row.dtype)])
    tiled_flat = jnp.tile(extended, row_count)[: row_count * (row_count + tap_count - 1)]
    return tiled_flat.reshape(row_count, row_count + tap_count - 1)


def fir_rows(padded_in, tap_row, row_count):
    tap_count = tap_row.shape[0]
    block_rows = min(512, row_count)
    toeplitz = band_matrix(tap_row, block_rows)
    partials = [
        jnp.dot(
            toeplitz,
            padded_in[offset : offset + block_rows + tap_count - 1],
            preferred_element_type=jnp.float32,
        )
        for offset in range(0, row_count, block_rows)
    ]
    return jnp.concatenate(partials, axis=0).astype(jnp.bfloat16)


def dynamic_filter(series, impulse, tap_limits):
    impulse_len = impulse.shape[1]
    kept_mask = jnp.arange(impulse_len, dtype=jnp.int32)[None, :] < tap_limits[:, None]
    kernel_taps = jnp.where(kept_mask, impulse, jnp.zeros_like(impulse))[:, ::-1]
    result = lax.conv_general_dilated(
        series[None],
        kernel_taps[:, None, :],
        window_strides=(1,),
        padding=[(impulse_len - 1, 0)],
        dimension_numbers=("NCH", "OIH", "NCH"),
        feature_group_count=series.shape[0],
        precision=lax.Precision.HIGHEST,
    )
    return result[0]


def score_block(responses, filtered, mean_panel, spread_panel):
    sample_count = filtered.shape[0]
    resp_wide = responses.astype(jnp.float32)
    mean_mode = jnp.mean(resp_wide, axis=1)
    spread_mode = jnp.sqrt(jnp.mean(jnp.square(resp_wide - mean_mode[:, None]), axis=1) + 1e-06)
    cross = jnp.dot(responses, filtered, preferred_element_type=jnp.float32)
    covariance = cross / sample_count - mean_mode[:, None] * mean_panel[None, :]
    return math.sqrt(sample_count) * covariance / (spread_mode[:, None] * spread_panel[None, :])


def body(pressure, fir_taps, influence, mode_impulse, mode_taps):
    tap_count = fir_taps.shape[0]
    regrouped = lax.all_to_all(pressure, "gx", split_axis=1, concat_axis=0, tiled=True)
    zero_rim = jnp.zeros((tap_count - 1, regrouped.shape[1]), regrouped.dtype)
    filtered = fir_rows(
        jnp.concatenate([zero_rim, regrouped], axis=0), fir_taps, regrouped.shape[0]
    )
    lines = influence.reshape(influence.shape[0], -1)
    mode_count = lines.shape[0]
    per_device = mode_count // lax.axis_size(("gx", "gy", "gz"))
    mean_panel = jnp.mean(filtered, axis=0, dtype=jnp.float32)
    spread_panel = jnp.sqrt(
        jnp.mean(jnp.square(filtered.astype(jnp.float32) - mean_panel[None, :]), axis=0) + 1e-06
    )
    first_mode = lax.axis_index(("gx", "gy", "gz")) * per_device
    own_loads = lax.psum_scatter(
        lax.dot_general(
            lines, filtered, (((1,), (1,)), ((), ())), preferred_element_type=jnp.float32
        ),
        ("gx", "gy", "gz"),
        scatter_dimension=0,
        tiled=True,
    )
    own_impulse = lax.dynamic_slice_in_dim(mode_impulse, first_mode, per_device, 0)
    own_limits = lax.dynamic_slice_in_dim(mode_taps, first_mode, per_device, 0)
    own_modes = dynamic_filter(own_loads, own_impulse, own_limits).astype(jnp.bfloat16)
    scores = score_block(
        lax.all_gather(own_modes, ("gx", "gy", "gz"), axis=0, tiled=True),
        filtered,
        mean_panel,
        spread_panel,
    )
    return (own_modes, scores.reshape(influence.shape))


def solution(mesh):
    return jax.shard_map(
        body,
        mesh=mesh,
        in_specs=(
            P(("wind", "gx"), ("gy", "gz")),
            P(),
            P(None, ("gy", "gz"), "gx", None),
            P(),
            P(),
        ),
        out_specs=(P(("wind", "gx", "gy", "gz"), None), P("wind", ("gy", "gz"), "gx", None)),
        check_vma=False,
    )
```

profile of v0, /device:TPU:0, one launch (start us, length us, event | category | flops | bytes accessed | tf_op | source)
XLA Modules:
  0.0 279.5 jit_solution(2012428702665789185)
XLA Ops:
  7.2 0.0 copy-start
  7.2 6.5 %copy.44 = bf16[1024,2048]{0,1:T(8,128)(2,1)} copy(bf16[1024,2048]{1,0:T(8,128)(2,1)} %param.5) | data formatting | bytes 8388608 | tf_op args[0]
  13.7 6.4 %all-to-all-start = ((bf16[1024,4,512]{0,2,1:T(8,128)(2,1)}), bf16[1024,4,512]{0,2,1:T(8,128)(2,1)}, u32[]{:S(2)}, u32[]{:S(2)}) async-start(bf16[1024,4,512]{0,2,1:T(8,128)(2,1)} %bitcast.53), calls=%async_computation | async-start | bytes 8388608 | tf_op jit(solution)/shard_map/all_to_all | solution.py:58
  20.1 0.0 reduce-scatter.4.cloned.1.call-start
  20.1 0.1 reverse
  20.2 0.1 slice.66
  20.3 0.1 tile.4
  20.4 1.3 tile.10
  21.7 0.1 slice.38
  21.8 0.7 reshape.35
  22.5 91.1 %all-to-all-done = bf16[1024,4,512]{0,2,1:T(8,128)(2,1)} async-done(((bf16[1024,4,512]{0,2,1:T(8,128)(2,1)}), bf16[1024,4,512]{0,2,1:T(8,128)(2,1)}, u32[]{:S(2)}, u32[]{:S(2)}) %all-to-all-start) | async-done | bytes 4194336 | tf_op jit(solution)/shard_map/all_to_all | solution.py:58
  113.6 6.2 %copy.45 = bf16[4,1024,512]{2,1,0:T(8,128)(2,1)} copy(bf16[4,1024,512]{1,2,0:T(8,128)(2,1)} %bitcast.1) | data formatting | bytes 8388608 | tf_op jit(solution)/shard_map/all_to_all | solution.py:58
  119.8 1.7 fusion.18
  121.5 0.6 copy-done.4
  122.1 0.6 fusion.17
  122.7 0.6 fusion.16
  123.3 0.6 fusion.15
  123.9 0.6 fusion.14
  124.4 0.6 fusion.13
  125.0 0.6 fusion.12
  125.6 0.6 fusion.11
  126.2 1.9 copy-done.1
  128.1 3.2 %convolution_bitcast_fusion = f32[256,4096]{0,1:T(8,128)} fusion(bf16[4096,512]{1,0:T(8,128)(2,1)S(1)} %fusion.11, bf16[256,1,1,512]{3,0,2,1:T(8,128)(2,1)S(1)} %copy-done), kind=kOutput, calls=%fused_computation.4 | convolution fusion | flops 1073741824 | bytes 8650752 | tf_op jit(solution)/shard_map/dot_general | solution.py:72
  131.3 5.6 %copy.56 = f32[256,4096]{1,0:T(8,128)} copy(f32[256,4096]{0,1:T(8,128)} %convolution_bitcast_fusion) | data formatting | bytes 8388608
  137.0 0.0 reduce-scatter.4.cloned.1.call-update
  137.0 0.2 all-gather.3.cloned.1.call-start
  137.2 0.4 copy-done.8
  137.7 0.1 dynamic_slice.6
  137.7 0.1 copy-done.5
  137.8 0.1 dynamic-slice_select_fusion
  137.9 70.8 %reduce-scatter.4.cloned.1.call-done = f32[16,4096]{1,0:T(8,128)} async-done(((f32[256,4096]{1,0:T(8,128)}), f32[16,4096]{1,0:T(8,128)}) %reduce-scatter.4.cloned.1.call-update) | async-done | bytes 262160
  208.7 1.5 copy.57
  210.3 0.2 pad.2
  210.5 0.4 copy.48
  210.9 0.0 copy-start.6
  211.0 10.8 %fusion.5 = bf16[8,520,16]{2,0,1:T(8,128)(2,1)S(1)} fusion(f32[16,1,64]{0,1,2:T(1,128)S(1)} %bitcast.64, f32[16,1,7,63]{0,2,3,1:T(8,128)S(1)} %slice.46, f32[16,1,8,520]{0,2,3,1:T(8,128)S(1)} %copy.48), kind=kOutput, calls=%fused_computation.12 | convolution fusion | flops 51341952 | bytes 431680 | tf_op jit(solution)/shard_map/conv_general_dilated | solution.py:34
  221.7 0.7 copy.50
  222.5 0.2 reshape.44
  222.7 0.7 slice_bitcast_fusion.1
  223.4 0.0 all-gather.3.cloned.1.call-update
  223.5 3.0 %convert_reduce_fusion = f32[512]{0:T(512)S(1)} fusion(bf16[4096,512]{1,0:T(8,128)(2,1)} %copy-done.1), kind=kLoop, calls=%fused_computation.1 | loop fusion | flops 4193792 | bytes 4196352 | tf_op jit(solution)/shard_map/reduce_sum | solution.py:66
  226.4 0.5 copy-done.2
  226.9 1.2 fusion.1
  228.1 35.9 %all-gather.3.cloned.1.call-done = bf16[1,256,4096]{2,1,0:T(8,128)(2,1)} async-done(((bf16[1,16,4096]{2,1,0:T(8,128)(2,1)}), bf16[1,256,4096]{2,1,0:T(8,128)(2,1)}) %all-gather.3.cloned.1.call-update) | async-done | bytes 2097168 | tf_op jit(solution)/shard_map/all_gather | solution.py:83
  264.0 2.1 convert_reduce_fusion.1
  266.1 2.3 fusion.3
  268.4 2.9 %fusion.33 = f32[256,1,1,512]{3,0,2,1:T(8,128)S(1)} fusion(bf16[4096,512]{1,0:T(8,128)(2,1)S(1)} %copy-done.3, bf16[1,256,4096]{2,1,0:T(8,128)(2,1)} %all-gather.3.cloned.1.call-done, f32[512]{0:T(512)S(1)} %add_sqrt_fusion, f32[256]{0:T(256)S(1)} %add_sqrt_fusion.1, f32[512]{0:T(512)S(1)} %broadcast_multiply_fusion, f32[256]{0:T(256)S(1)} %broadcast_multiply_fusion.1), kind=kOutput, calls=%fused_computation.40 | convolution fusion | flops 1074528256 | bytes 6821888 | tf_op jit(solution)/shard_map/dot_general | solution.py:51
  271.3 1.3 copy.52
  (20 shorter events, 0.2 us)
Async XLA Ops:
  7.2 120.9 %copy-start = (bf16[256,1,1,512]{3,0,2,1:T(8,128)(2,1)S(1)}, bf16[256,1,1,512]{3,0,2,1:T(8,128)(2,1)}, u32[]{:S(2)}) copy-start(bf16[256,1,1,512]{3,0,2,1:T(8,128)(2,1)} %param.7) | copy-start | bytes 786436
  13.7 6.5 %copy-start.7 = (bf16[257]{0:T(512)(128)(2,1)S(1)}, bf16[257]{0:T(512)(128)(2,1)}, u32[]{:S(2)}) copy-start(bf16[257]{0:T(512)(128)(2,1)} %param.6) | copy-start | bytes 1546
  13.7 99.9 %all-to-all-start = ((bf16[1024,4,512]{0,2,1:T(8,128)(2,1)}), bf16[1024,4,512]{0,2,1:T(8,128)(2,1)}, u32[]{:S(2)}, u32[]{:S(2)}) async-start(bf16[1024,4,512]{0,2,1:T(8,128)(2,1)} %bitcast.53), calls=%async_computation | async-start | bytes 8388608 | tf_op jit(solution)/shard_map/all_to_all | solution.py:58
  20.1 188.6 %reduce-scatter.4.cloned.1.call-start = ((), (), s32[]{:S(2)}) async-start(), calls=%async_computation.3 | async-start | bytes 4456448
  119.8 2.3 copy-start.4
  126.2 1.9 copy-start.1
  137.0 0.7 copy-start.8
  137.0 0.9 copy-start.5
  137.0 127.0 %all-gather.3.cloned.1.call-start = ((), (), s32[]{:S(2)}) async-start(), calls=%async_computation.2 | async-start | bytes 2228224 | tf_op jit(solution)/shard_map/all_gather | solution.py:83
  210.9 11.5 %copy-start.6 = (pred[8,520]{1,0:T(8,128)(4,1)S(1)}, pred[8,520]{1,0:T(8,128)(4,1)}, u32[]{:S(2)}) copy-start(pred[8,520]{1,0:T(8,128)(4,1)} %constant.52) | copy-start | bytes 12484
  223.4 3.5 %copy-start.2 = (bf16[4096,512]{1,0:T(8,128)(2,1)S(1)}, bf16[4096,512]{1,0:T(8,128)(2,1)}, u32[]{:S(2)}) copy-start(bf16[4096,512]{1,0:T(8,128)(2,1)} %copy-done.1) | copy-start | bytes 12582916
  264.0 4.4 %copy-start.3 = (bf16[4096,512]{1,0:T(8,128)(2,1)S(1)}, bf16[4096,512]{1,0:T(8,128)(2,1)}, u32[]{:S(2)}) copy-start(bf16[4096,512]{1,0:T(8,128)(2,1)} %copy-done.1) | copy-start | bytes 12582916
Sparse Core Ops, SparseCore 0:
  137.1 71.5 reduce-scatter.3
  223.6 40.3 all-gather.2
where the time goes:
time: 280 us
  waiting for transfers between devices  198 us (71%)
  local copies, waits for them, and re-layouts  29.5 us (11%)
  matrix products  22.6 us (8%)
  between operations  14.2 us (5%)
  other arithmetic  8.64 us (3%)
  starting transfers between devices  6.67 us (2%)
    all_to_all x1, waiting for transfers between devices, body(): lax.all_to_all(pressure, 'gx', split_axis=1, concat_axis=0, tiled=True)  91.1 us
    unnamed x3, waiting for transfers between devices  70.8 us
    all_gather x1, waiting for transfers between devices, body(): lax.all_gather(own_modes, ('gx', 'gy', 'gz'), axis=0, tiled=True)  35.9 us
    unnamed x24, local copies, waits for them, and re-layouts  18.8 us
    conv_general_dilated x1, matrix products, dynamic_filter(): lax.conv_general_dilated(series[None], kernel_taps[:, None, :], window_st...  10.8 us
    all_to_all x1, starting transfers between devices, body(): lax.all_to_all(pressure, 'gx', split_axis=1, concat_axis=0, tiled=True)  6.45 us
    all_to_all x1, local copies, waits for them, and re-layouts, body(): lax.all_to_all(pressure, 'gx', split_axis=1, concat_axis=0, tiled=True)  6.23 us
    dot_general x8, matrix products, fir_rows(): jnp.dot(toeplitz, padded_in[offset:offset + block_rows + tap_count - 1],...  5.71 us
  transfers between devices with their start and end apart: 3, of which 3 were waited for; matrix products, arithmetic and copies ran while one was open for 2% of the time, Pallas kernels for 0%

commit v1 on v0

--- a/solution.py
+++ b/solution.py
@@ -3,6 +3,12 @@
 import jax.numpy as jnp
 from jax import lax
 from jax.sharding import PartitionSpec as P
+
+
+def _put_rows(z_in, where_dim):
+    z_in = jnp.moveaxis(z_in, 0, where_dim)
+    y2 = z_in.shape
+    return z_in.reshape(*y2[:where_dim], y2[where_dim] * y2[where_dim + 1], *y2[where_dim + 2 :])
 
 
 def band_matrix(tap_row, row_count):
@@ -79,11 +85,28 @@
     own_impulse = lax.dynamic_slice_in_dim(mode_impulse, first_mode, per_device, 0)
     own_limits = lax.dynamic_slice_in_dim(mode_taps, first_mode, per_device, 0)
     own_modes = dynamic_filter(own_loads, own_impulse, own_limits).astype(jnp.bfloat16)
+
+    def proceed_stops_all(mat, group_axis, ndim_at):
+        full_n = lax.axis_size(group_axis)
+        made = tuple(((dev_i, (dev_i + 1) % full_n) for dev_i in range(full_n)))
+        pieces_in = tuple(((no, dd) for dd, no in made))
+        z, val = ([], [])
+        for at in range(full_n - 1):
+            if at % 2 == 0:
+                block_now = lax.ppermute(z[-1] if z else mat, group_axis, made)
+                z.append(block_now)
+            else:
+                latest = lax.ppermute(val[-1] if val else mat, group_axis, pieces_in)
+                val.append(latest)
+        earlier = jnp.stack([*z[::-1], mat, *val])
+        seen_now = lax.axis_index(group_axis)
+        step_out = len(z)
+        side_arr = seen_now - step_out
+        earlier = earlier[(jnp.arange(full_n) - side_arr) % full_n]
+        return _put_rows(earlier, ndim_at)
+
     scores = score_block(
-        lax.all_gather(own_modes, ("gx", "gy", "gz"), axis=0, tiled=True),
-        filtered,
-        mean_panel,
-        spread_panel,
+        proceed_stops_all(own_modes, ("gx", "gy", "gz"), 0), filtered, mean_panel, spread_panel
     )
     return (own_modes, scores.reshape(influence.shape))
 

time: 280 us -> 307 us (1.096)
  starting transfers between devices: 6.67 us -> 38.1 us
  waiting for transfers between devices: 198 us -> 184 us
  local copies, waits for them, and re-layouts: 29.5 us -> 41.7 us
  other arithmetic: 8.64 us -> 5.17 us
    all_gather x1 -> x0, waiting for transfers between devices: 35.9 us -> none  [body(): lax.all_gather(own_modes, ('gx', 'gy', 'gz'), axis=0, tiled=True)]
    ppermute x0 -> x15, starting transfers between devices: none -> 31.6 us  [the longest x7 31.6 us: proceed_stops_all(): latest = lax.ppermute(val[-1] if val else mat, group_axis, pieces_in)]
    ppermute x0 -> x15, waiting for transfers between devices: none -> 21.5 us  [the longest x8 15.1 us: proceed_stops_all(): block_now = lax.ppermute(z[-1] if z else mat, group_axis, made)]
    unnamed x24 -> x39, local copies, waits for them, and re-layouts: 18.8 us -> 28.6 us
    unnamed x3 -> x2, waiting for transfers between devices: 70.8 us -> 71.1 us
  transfers between devices with their start and end apart: 3 -> 17, of which waited for: 3 -> 9; matrix products, arithmetic and copies ran while one was open for 2% -> 5% of each run, Pallas kernels for 0% -> 0%
where the time goes in v1:
time: 307 us; the launch traced here: 306 us
  waiting for transfers between devices  184 us (60%)
  local copies, waits for them, and re-layouts  41.7 us (14%)
  starting transfers between devices  38.1 us (12%)
  matrix products  23.2 us (8%)
  between operations  14.3 us (5%)
  other arithmetic  5.17 us (2%)
    all_to_all x1, waiting for transfers between devices, body(): lax.all_to_all(pressure, 'gx', split_axis=1, concat_axis=0, tiled=True)  91.1 us
    unnamed x2, waiting for transfers between devices  71.1 us
    ppermute x7, starting transfers between devices, proceed_stops_all(): latest = lax.ppermute(val[-1] if val else mat, group_axis, pieces_in)  31.6 us
    unnamed x39, local copies, waits for them, and re-layouts  28.6 us
    ppermute x8, waiting for transfers between devices, proceed_stops_all(): block_now = lax.ppermute(z[-1] if z else mat, group_axis, made)  15.1 us
    conv_general_dilated x1, matrix products, dynamic_filter(): lax.conv_general_dilated(series[None], kernel_taps[:, None, :], window_st...  10.8 us
    all_to_all x1, starting transfers between devices, body(): lax.all_to_all(pressure, 'gx', split_axis=1, concat_axis=0, tiled=True)  6.45 us
    ppermute x7, waiting for transfers between devices, proceed_stops_all(): latest = lax.ppermute(val[-1] if val else mat, group_axis, pieces_in)  6.38 us
  transfers between devices with their start and end apart: 17, of which 9 were waited for; matrix products, arithmetic and copies ran while one was open for 5% of the time, Pallas kernels for 0%

profile of v1, /device:TPU:0, one launch (start us, length us, event | category | flops | bytes accessed | tf_op | source)
XLA Modules:
  0.0 306.2 jit_solution(4877843184902249684)
XLA Ops:
  7.2 6.5 %copy.44 = bf16[1024,2048]{0,1:T(8,128)(2,1)} copy(bf16[1024,2048]{1,0:T(8,128)(2,1)} %param.5) | data formatting | bytes 8388608 | tf_op args[0]
  13.7 6.4 %all-to-all-start = ((bf16[1024,4,512]{0,2,1:T(8,128)(2,1)}), bf16[1024,4,512]{0,2,1:T(8,128)(2,1)}, u32[]{:S(2)}, u32[]{:S(2)}) async-start(bf16[1024,4,512]{0,2,1:T(8,128)(2,1)} %bitcast.73), calls=%async_computation | async-start | bytes 8388608 | tf_op jit(solution)/shard_map/all_to_all | solution.py:64
  20.4 1.3 tile.10
  21.8 0.7 reshape.107
  22.5 91.1 %all-to-all-done = bf16[1024,4,512]{0,2,1:T(8,128)(2,1)} async-done(((bf16[1024,4,512]{0,2,1:T(8,128)(2,1)}), bf16[1024,4,512]{0,2,1:T(8,128)(2,1)}, u32[]{:S(2)}, u32[]{:S(2)}) %all-to-all-start) | async-done | bytes 4194336 | tf_op jit(solution)/shard_map/all_to_all | solution.py:64
  113.5 6.2 %copy.45 = bf16[4,1024,512]{2,1,0:T(8,128)(2,1)} copy(bf16[4,1024,512]{1,2,0:T(8,128)(2,1)} %bitcast.1) | data formatting | bytes 8388608 | tf_op jit(solution)/shard_map/all_to_all | solution.py:64
  119.8 1.7 fusion.16
  126.1 1.9 copy-done.1
  128.1 3.3 %convolution_bitcast_fusion = f32[256,4096]{0,1:T(8,128)} fusion(bf16[4096,512]{1,0:T(8,128)(2,1)S(1)} %fusion.9, bf16[256,1,1,512]{3,0,2,1:T(8,128)(2,1)S(1)} %copy-done), kind=kOutput, calls=%fused_computation.5 | convolution fusion | flops 1073741824 | bytes 8650752 | tf_op jit(solution)/shard_map/dot_general | solution.py:78
  131.3 5.7 %copy.56 = f32[256,4096]{1,0:T(8,128)} copy(f32[256,4096]{0,1:T(8,128)} %convolution_bitcast_fusion) | data formatting | bytes 8388608
  138.0 71.1 %reduce-scatter.4.cloned.1.call-done = f32[16,4096]{1,0:T(8,128)} async-done(((f32[256,4096]{1,0:T(8,128)}), f32[16,4096]{1,0:T(8,128)}) %reduce-scatter.4.cloned.1.call-update) | async-done | bytes 262160
  209.1 1.5 copy.57
  211.3 10.8 %fusion.5 = bf16[8,520,16]{2,0,1:T(8,128)(2,1)S(1)} fusion(f32[16,1,64]{0,1,2:T(1,128)S(1)} %bitcast.84, f32[16,1,7,63]{0,2,3,1:T(8,128)S(1)} %slice.48, f32[16,1,8,520]{0,2,3,1:T(8,128)S(1)} %copy.48), kind=kOutput, calls=%fused_computation.13 | convolution fusion | flops 51341952 | bytes 431680 | tf_op jit(solution)/shard_map/conv_general_dilated | solution.py:40
  222.1 0.7 copy.50
  223.2 7.1 %collective-permute-done = bf16[16,4096]{1,0:T(8,128)(2,1)S(1)} collective-permute-done((bf16[16,4096]{1,0:T(8,128)(2,1)S(1)}, bf16[16,4096]{1,0:T(8,128)(2,1)S(1)}, u32[]{:S(2)}, u32[]{:S(2)}) %collective-permute-start) | collective-permute-done | bytes 131104 | tf_op jit(solution)/shard_map/ppermute | solution.py:96
  230.2 4.4 %collective-permute-start.8 = (bf16[16,4096]{1,0:T(8,128)(2,1)S(1)}, bf16[16,4096]{1,0:T(8,128)(2,1)S(1)}, u32[]{:S(2)}, u32[]{:S(2)}) collective-permute-start(bf16[16,4096]{1,0:T(8,128)(2,1)S(1)} %slice_bitcast_fusion), channel_id=1, source_target_pairs={{1,0},{2,1},{3,2},{4,3},{5,4},{6,5},{7,6},{8,7},{9,8},{10,9},{11,1... | collective-permute-start | bytes 393224 | tf_op jit(solution)/shard_map/ppermute | solution.py:99
  234.7 2.8 collective-permute-done.1
  237.5 4.4 %collective-permute-start.9 = (bf16[16,4096]{1,0:T(8,128)(2,1)S(1)}, bf16[16,4096]{1,0:T(8,128)(2,1)S(1)}, u32[]{:S(2)}, u32[]{:S(2)}) collective-permute-start(bf16[16,4096]{1,0:T(8,128)(2,1)S(1)} %collective-permute-done.8), channel_id=1, source_target_pairs={{1,0},{2,1},{3,2},{4,3},{5,4},{6,5},{7,6},{8,7},{9,8},{10,9},{11,1... | collective-permute-start | bytes 393224 | tf_op jit(solution)/shard_map/ppermute | solution.py:99
  241.9 2.7 collective-permute-done.2
  244.7 4.5 %collective-permute-start.10 = (bf16[16,4096]{1,0:T(8,128)(2,1)S(1)}, bf16[16,4096]{1,0:T(8,128)(2,1)S(1)}, u32[]{:S(2)}, u32[]{:S(2)}) collective-permute-start(bf16[16,4096]{1,0:T(8,128)(2,1)S(1)} %collective-permute-done.9), channel_id=1, source_target_pairs={{1,0},{2,1},{3,2},{4,3},{5,4},{6,5},{7,6},{8,7},{9,8},{10,9},{11,1... | collective-permute-start | bytes 393224 | tf_op jit(solution)/shard_map/ppermute | solution.py:99
  249.2 2.6 collective-permute-done.3
  251.7 2.8 convert_reduce_fusion
  254.5 4.5 %collective-permute-start.11 = (bf16[16,4096]{1,0:T(8,128)(2,1)S(1)}, bf16[16,4096]{1,0:T(8,128)(2,1)S(1)}, u32[]{:S(2)}, u32[]{:S(2)}) collective-permute-start(bf16[16,4096]{1,0:T(8,128)(2,1)S(1)} %collective-permute-done.10), channel_id=1, source_target_pairs={{1,0},{2,1},{3,2},{4,3},{5,4},{6,5},{7,6},{8,7},{9,8},{10,9},{11,1... | collective-permute-start | bytes 393224 | tf_op jit(solution)/shard_map/ppermute | solution.py:99
  259.0 2.5 collective-permute-done.11
  261.6 4.6 %collective-permute-start.12 = (bf16[16,4096]{1,0:T(8,128)(2,1)S(1)}, bf16[16,4096]{1,0:T(8,128)(2,1)S(1)}, u32[]{:S(2)}, u32[]{:S(2)}) collective-permute-start(bf16[16,4096]{1,0:T(8,128)(2,1)S(1)} %collective-permute-done.11), channel_id=1, source_target_pairs={{1,0},{2,1},{3,2},{4,3},{5,4},{6,5},{7,6},{8,7},{9,8},{10,9},{11,1... | collective-permute-start | bytes 393224 | tf_op jit(solution)/shard_map/ppermute | solution.py:99
  266.1 1.2 fusion.1
  267.3 1.4 collective-permute-done.12
  268.6 4.6 %collective-permute-start.13 = (bf16[16,4096]{1,0:T(8,128)(2,1)S(1)}, bf16[16,4096]{1,0:T(8,128)(2,1)S(1)}, u32[]{:S(2)}, u32[]{:S(2)}) collective-permute-start(bf16[16,4096]{1,0:T(8,128)(2,1)S(1)} %collective-permute-done.12), channel_id=1, source_target_pairs={{1,0},{2,1},{3,2},{4,3},{5,4},{6,5},{7,6},{8,7},{9,8},{10,9},{11,1... | collective-permute-start | bytes 393224 | tf_op jit(solution)/shard_map/ppermute | solution.py:99
  273.2 2.5 collective-permute-done.13
  275.7 4.6 %collective-permute-start.14 = (bf16[16,4096]{1,0:T(8,128)(2,1)S(1)}, bf16[16,4096]{1,0:T(8,128)(2,1)S(1)}, u32[]{:S(2)}, u32[]{:S(2)}) collective-permute-start(bf16[16,4096]{1,0:T(8,128)(2,1)S(1)} %collective-permute-done.13), channel_id=1, source_target_pairs={{1,0},{2,1},{3,2},{4,3},{5,4},{6,5},{7,6},{8,7},{9,8},{10,9},{11,1... | collective-permute-start | bytes 393224 | tf_op jit(solution)/shard_map/ppermute | solution.py:99
  280.3 0.7 bitcast_dynamic-update-slice_fusion.14
  281.0 0.7 bitcast_dynamic-update-slice_fusion.13
  281.6 0.7 bitcast_dynamic-update-slice_fusion.12
  283.0 0.7 bitcast_dynamic-update-slice_fusion.10
  283.6 0.7 bitcast_dynamic-update-slice_fusion.9
  284.3 0.7 bitcast_dynamic-update-slice_fusion.8
  285.0 0.7 bitcast_dynamic-update-slice_fusion.7
  285.7 0.7 bitcast_dynamic-update-slice_fusion.15
  286.3 0.7 bitcast_dynamic-update-slice_fusion.6
  287.0 0.7 bitcast_dynamic-update-slice_fusion.5
  287.7 0.7 bitcast_dynamic-update-slice_fusion.4
  288.4 0.7 bitcast_dynamic-update-slice_fusion.3
  289.0 0.7 bitcast_dynamic-update-slice_fusion.2
  290.4 0.7 bitcast_dynamic-update-slice_fusion
  291.0 2.3 gather_fusion
  293.7 0.7 fusion.3
  294.6 3.5 %fusion.22 = f32[256,1,1,512]{3,0,2,1:T(8,128)S(1)} fusion(bf16[256,4096]{1,0:T(8,128)(2,1)S(1)} %bitcast.72, bf16[4096,512]{1,0:T(8,128)(2,1)} %copy-done.1, f32[512]{0:T(512)S(1)} %add_sqrt_fusion.1, f32[256]{0:T(256)S(1)} %sqrt.18, f32[512]{0:T(512)S(1)} %broadcast_multiply_fusion.1, f32[256]{0:T(256)S(1)} %div.26), kind=kOutput, calls=%fused_computation.39 | convolution fusion | flops 1074528256 | bytes 6821888 | tf_op jit(solution)/shard_map/dot_general | solution.py:57
  298.0 1.3 copy.52
  (68 shorter events, 8.7 us)
Async XLA Ops:
  7.2 120.9 %copy-start = (bf16[256,1,1,512]{3,0,2,1:T(8,128)(2,1)S(1)}, bf16[256,1,1,512]{3,0,2,1:T(8,128)(2,1)}, u32[]{:S(2)}) copy-start(bf16[256,1,1,512]{3,0,2,1:T(8,128)(2,1)} %param.7) | copy-start | bytes 786436
  13.6 6.5 %copy-start.7 = (bf16[257]{0:T(512)(128)(2,1)S(1)}, bf16[257]{0:T(512)(128)(2,1)}, u32[]{:S(2)}) copy-start(bf16[257]{0:T(512)(128)(2,1)} %param.6) | copy-start | bytes 1546
  13.7 99.9 %all-to-all-start = ((bf16[1024,4,512]{0,2,1:T(8,128)(2,1)}), bf16[1024,4,512]{0,2,1:T(8,128)(2,1)}, u32[]{:S(2)}, u32[]{:S(2)}) async-start(bf16[1024,4,512]{0,2,1:T(8,128)(2,1)} %bitcast.73), calls=%async_computation | async-start | bytes 8388608 | tf_op jit(solution)/shard_map/all_to_all | solution.py:64
  20.1 189.0 %reduce-scatter.4.cloned.1.call-start = ((), (), s32[]{:S(2)}) async-start(), calls=%async_computation.2 | async-start | bytes 4456448
  119.8 2.3 copy-start.3
  126.1 1.9 copy-start.1
  137.0 0.7 copy-start.8
  137.0 0.9 copy-start.5
  211.3 11.5 %copy-start.6 = (pred[8,520]{1,0:T(8,128)(4,1)S(1)}, pred[8,520]{1,0:T(8,128)(4,1)}, u32[]{:S(2)}) copy-start(pred[8,520]{1,0:T(8,128)(4,1)} %constant.69) | copy-start | bytes 12484
  223.1 44.2 %copy-start.4 = (bf16[16,4096]{1,0:T(8,128)(2,1)}, bf16[16,4096]{1,0:T(8,128)(2,1)S(1)}, u32[]{:S(2)}) copy-start(bf16[16,4096]{1,0:T(8,128)(2,1)S(1)} %slice_bitcast_fusion) | copy-start | bytes 393220
  223.1 7.1 %collective-permute-start = (bf16[16,4096]{1,0:T(8,128)(2,1)S(1)}, bf16[16,4096]{1,0:T(8,128)(2,1)S(1)}, u32[]{:S(2)}, u32[]{:S(2)}) collective-permute-start(bf16[16,4096]{1,0:T(8,128)(2,1)S(1)} %slice_bitcast_fusion), channel_id=1, source_target_pairs={{0,1},{1,2},{2,3},{3,4},{4,5},{5,6},{6,7},{7,8},{8,9},{9,10},{10,1... | collective-permute-start | bytes 393224 | tf_op jit(solution)/shard_map/ppermute | solution.py:96
  230.2 7.2 %collective-permute-start.1 = (bf16[16,4096]{1,0:T(8,128)(2,1)S(1)}, bf16[16,4096]{1,0:T(8,128)(2,1)S(1)}, u32[]{:S(2)}, u32[]{:S(2)}) collective-permute-start(bf16[16,4096]{1,0:T(8,128)(2,1)S(1)} %collective-permute-done), channel_id=1, source_target_pairs={{0,1},{1,2},{2,3},{3,4},{4,5},{5,6},{6,7},{7,8},{8,9},{9,10},{10,1... | collective-permute-start | bytes 393224 | tf_op jit(solution)/shard_map/ppermute | solution.py:96
  230.2 7.2 %collective-permute-start.8 = (bf16[16,4096]{1,0:T(8,128)(2,1)S(1)}, bf16[16,4096]{1,0:T(8,128)(2,1)S(1)}, u32[]{:S(2)}, u32[]{:S(2)}) collective-permute-start(bf16[16,4096]{1,0:T(8,128)(2,1)S(1)} %slice_bitcast_fusion), channel_id=1, source_target_pairs={{1,0},{2,1},{3,2},{4,3},{5,4},{6,5},{7,6},{8,7},{9,8},{10,9},{11,1... | collective-permute-start | bytes 393224 | tf_op jit(solution)/shard_map/ppermute | solution.py:99
  237.4 7.2 %collective-permute-start.2 = (bf16[16,4096]{1,0:T(8,128)(2,1)S(1)}, bf16[16,4096]{1,0:T(8,128)(2,1)S(1)}, u32[]{:S(2)}, u32[]{:S(2)}) collective-permute-start(bf16[16,4096]{1,0:T(8,128)(2,1)S(1)} %collective-permute-done.1), channel_id=1, source_target_pairs={{0,1},{1,2},{2,3},{3,4},{4,5},{5,6},{6,7},{7,8},{8,9},{9,10},{10,1... | collective-permute-start | bytes 393224 | tf_op jit(solution)/shard_map/ppermute | solution.py:96
  237.4 28.7 %copy-start.2 = (bf16[4096,512]{1,0:T(8,128)(2,1)S(1)}, bf16[4096,512]{1,0:T(8,128)(2,1)}, u32[]{:S(2)}) copy-start(bf16[4096,512]{1,0:T(8,128)(2,1)} %copy-done.1) | copy-start | bytes 12582916
  237.5 7.2 %collective-permute-start.9 = (bf16[16,4096]{1,0:T(8,128)(2,1)S(1)}, bf16[16,4096]{1,0:T(8,128)(2,1)S(1)}, u32[]{:S(2)}, u32[]{:S(2)}) collective-permute-start(bf16[16,4096]{1,0:T(8,128)(2,1)S(1)} %collective-permute-done.8), channel_id=1, source_target_pairs={{1,0},{2,1},{3,2},{4,3},{5,4},{6,5},{7,6},{8,7},{9,8},{10,9},{11,1... | collective-permute-start | bytes 393224 | tf_op jit(solution)/shard_map/ppermute | solution.py:99
  244.6 7.1 %collective-permute-start.3 = (bf16[16,4096]{1,0:T(8,128)(2,1)S(1)}, bf16[16,4096]{1,0:T(8,128)(2,1)S(1)}, u32[]{:S(2)}, u32[]{:S(2)}) collective-permute-start(bf16[16,4096]{1,0:T(8,128)(2,1)S(1)} %collective-permute-done.2), channel_id=1, source_target_pairs={{0,1},{1,2},{2,3},{3,4},{4,5},{5,6},{6,7},{7,8},{8,9},{9,10},{10,1... | collective-permute-start | bytes 393224 | tf_op jit(solution)/shard_map/ppermute | solution.py:96
  244.7 9.9 %collective-permute-start.10 = (bf16[16,4096]{1,0:T(8,128)(2,1)S(1)}, bf16[16,4096]{1,0:T(8,128)(2,1)S(1)}, u32[]{:S(2)}, u32[]{:S(2)}) collective-permute-start(bf16[16,4096]{1,0:T(8,128)(2,1)S(1)} %collective-permute-done.9), channel_id=1, source_target_pairs={{1,0},{2,1},{3,2},{4,3},{5,4},{6,5},{7,6},{8,7},{9,8},{10,9},{11,1... | collective-permute-start | bytes 393224 | tf_op jit(solution)/shard_map/ppermute | solution.py:99
  251.7 7.3 %collective-permute-start.4 = (bf16[16,4096]{1,0:T(8,128)(2,1)S(1)}, bf16[16,4096]{1,0:T(8,128)(2,1)S(1)}, u32[]{:S(2)}, u32[]{:S(2)}) collective-permute-start(bf16[16,4096]{1,0:T(8,128)(2,1)S(1)} %collective-permute-done.3), channel_id=1, source_target_pairs={{0,1},{1,2},{2,3},{3,4},{4,5},{5,6},{6,7},{7,8},{8,9},{9,10},{10,1... | collective-permute-start | bytes 393224 | tf_op jit(solution)/shard_map/ppermute | solution.py:96
  254.5 7.0 %collective-permute-start.11 = (bf16[16,4096]{1,0:T(8,128)(2,1)S(1)}, bf16[16,4096]{1,0:T(8,128)(2,1)S(1)}, u32[]{:S(2)}, u32[]{:S(2)}) collective-permute-start(bf16[16,4096]{1,0:T(8,128)(2,1)S(1)} %collective-permute-done.10), channel_id=1, source_target_pairs={{1,0},{2,1},{3,2},{4,3},{5,4},{6,5},{7,6},{8,7},{9,8},{10,9},{11,1... | collective-permute-start | bytes 393224 | tf_op jit(solution)/shard_map/ppermute | solution.py:99
  259.0 7.1 %collective-permute-start.5 = (bf16[16,4096]{1,0:T(8,128)(2,1)S(1)}, bf16[16,4096]{1,0:T(8,128)(2,1)S(1)}, u32[]{:S(2)}, u32[]{:S(2)}) collective-permute-start(bf16[16,4096]{1,0:T(8,128)(2,1)S(1)} %collective-permute-done.4), channel_id=1, source_target_pairs={{0,1},{1,2},{2,3},{3,4},{4,5},{5,6},{6,7},{7,8},{8,9},{9,10},{10,1... | collective-permute-start | bytes 393224 | tf_op jit(solution)/shard_map/ppermute | solution.py:96
  261.6 7.1 %collective-permute-start.12 = (bf16[16,4096]{1,0:T(8,128)(2,1)S(1)}, bf16[16,4096]{1,0:T(8,128)(2,1)S(1)}, u32[]{:S(2)}, u32[]{:S(2)}) collective-permute-start(bf16[16,4096]{1,0:T(8,128)(2,1)S(1)} %collective-permute-done.11), channel_id=1, source_target_pairs={{1,0},{2,1},{3,2},{4,3},{5,4},{6,5},{7,6},{8,7},{9,8},{10,9},{11,1... | collective-permute-start | bytes 393224 | tf_op jit(solution)/shard_map/ppermute | solution.py:99
  266.1 7.1 %collective-permute-start.6 = (bf16[16,4096]{1,0:T(8,128)(2,1)S(1)}, bf16[16,4096]{1,0:T(8,128)(2,1)S(1)}, u32[]{:S(2)}, u32[]{:S(2)}) collective-permute-start(bf16[16,4096]{1,0:T(8,128)(2,1)S(1)} %collective-permute-done.5), channel_id=1, source_target_pairs={{0,1},{1,2},{2,3},{3,4},{4,5},{5,6},{6,7},{7,8},{8,9},{9,10},{10,1... | collective-permute-start | bytes 393224 | tf_op jit(solution)/shard_map/ppermute | solution.py:96
  268.6 7.1 %collective-permute-start.13 = (bf16[16,4096]{1,0:T(8,128)(2,1)S(1)}, bf16[16,4096]{1,0:T(8,128)(2,1)S(1)}, u32[]{:S(2)}, u32[]{:S(2)}) collective-permute-start(bf16[16,4096]{1,0:T(8,128)(2,1)S(1)} %collective-permute-done.12), channel_id=1, source_target_pairs={{1,0},{2,1},{3,2},{4,3},{5,4},{6,5},{7,6},{8,7},{9,8},{10,9},{11,1... | collective-permute-start | bytes 393224 | tf_op jit(solution)/shard_map/ppermute | solution.py:99
  273.2 7.1 %collective-permute-start.7 = (bf16[16,4096]{1,0:T(8,128)(2,1)S(1)}, bf16[16,4096]{1,0:T(8,128)(2,1)S(1)}, u32[]{:S(2)}, u32[]{:S(2)}) collective-permute-start(bf16[16,4096]{1,0:T(8,128)(2,1)S(1)} %collective-permute-done.6), channel_id=1, source_target_pairs={{0,1},{1,2},{2,3},{3,4},{4,5},{5,6},{6,7},{7,8},{8,9},{9,10},{10,1... | collective-permute-start | bytes 393224 | tf_op jit(solution)/shard_map/ppermute | solution.py:96
  275.7 14.6 %collective-permute-start.14 = (bf16[16,4096]{1,0:T(8,128)(2,1)S(1)}, bf16[16,4096]{1,0:T(8,128)(2,1)S(1)}, u32[]{:S(2)}, u32[]{:S(2)}) collective-permute-start(bf16[16,4096]{1,0:T(8,128)(2,1)S(1)} %collective-permute-done.13), channel_id=1, source_target_pairs={{1,0},{2,1},{3,2},{4,3},{5,4},{6,5},{7,6},{8,7},{9,8},{10,9},{11,1... | collective-permute-start | bytes 393224 | tf_op jit(solution)/shard_map/ppermute | solution.py:99
Sparse Core Ops, SparseCore 0:
  137.2 71.8 reduce-scatter.3
